TPU v7x, 256 devices: a whole 4x4x8 slice. The times are simulated.
256 devices in a mesh: chan: 32 (over y, z), day: 8 (over x, core).
Axes of the slice: x: 4, y: 4, z: 8, core: 2. Of those that a mesh axis runs over, the one named last changes fastest.
Arguments:
- segment_records: bfloat16 [16, 512, 24, 2048], P('day', 'chan')
- block_requests: int32 [32, 32, 2], replicated, may hold values from 0 to 15, as said below
- pair_slots: int32 [2048, 2], P('chan'), may hold values from 0 to 63, as said below
Outputs:
- correlations: float32 [2048, 256], P(('chan', 'day'))
Inputs may be any that keep to these rules, and one draw needn't show every extreme that they name: `block_requests`: for each owner and each device of chan, 2 different channels of that device, as indices among its 16 channels. `pair_slots`: rows 64 * o to 64 * (o + 1) - 1 are the pairs of owner o; an entry is a slot s * 2 + k of that owner, the k-th channel it requests from device s of chan; the two slots of a pair differ.
All inputs are finite; a program needn't handle non-finite values.
Results may differ from a plain program's by a relative error of at most 0.0051.
Values may be sent and summed in bfloat16 or wider, within the bound.
A program may use at most 256 MiB of HBM per device.

v0:
```python
import math

import jax
import jax.numpy as jnp
from jax import lax
from jax.sharding import PartitionSpec as P

L = 2048
F = 1024
LAGS = 256


def forward_table():
    sample_idx = jnp.arange(L, dtype=jnp.int32)[:, None]
    bin_idx = jnp.arange(1, F + 1, dtype=jnp.int32)[None, :]
    phase = (sample_idx * bin_idx % L).astype(jnp.float32) * (2.0 * math.pi / L)
    taper = 0.5 - 0.5 * jnp.cos(
        jnp.arange(L, dtype=jnp.int32).astype(jnp.float32) * (2.0 * math.pi / L)
    )
    table = jnp.concatenate(
        [taper[:, None] * jnp.cos(phase), -taper[:, None] * jnp.sin(phase)], axis=1
    )
    return table.astype(jnp.bfloat16)


def lag_table():
    bin_idx = jnp.arange(1, F + 1, dtype=jnp.int32)[:, None]
    lag_idx = jnp.arange(LAGS, dtype=jnp.int32)[None, :] - LAGS // 2
    phase = (bin_idx * lag_idx % L).astype(jnp.float32) * (2.0 * math.pi / L)
    return jnp.concatenate([jnp.cos(phase), -jnp.sin(phase)], axis=0)


def whiten(spectra):
    power = jnp.mean(spectra * spectra, axis=-1, keepdims=True)
    real_part = spectra[..., :F]
    imag_part = spectra[..., F:]
    amplitude = jnp.sqrt(real_part * real_part + imag_part * imag_part + 0.02 * power + 1e-06)
    return jnp.concatenate([real_part / amplitude, imag_part / amplitude], axis=-1).astype(
        jnp.bfloat16
    )


def cross_parts(left_spec, right_spec):
    left_full = left_spec.astype(jnp.float32)
    right_full = right_spec.astype(jnp.float32)
    left_real, left_imag = (left_full[..., :F], left_full[..., F:])
    right_real, right_imag = (right_full[..., :F], right_full[..., F:])
    real_part = jnp.sum(left_real * right_real + left_imag * right_imag, axis=2)
    imag_part = jnp.sum(left_imag * right_real - left_real * right_imag, axis=2)
    return jnp.concatenate([real_part, imag_part], axis=-1)


def body(segment_records, block_requests, pair_slots):
    day_dev, ch_dev, seg_count, length = segment_records.shape
    spectra = jnp.dot(
        segment_records.reshape(-1, length), forward_table(), preferred_element_type=jnp.float32
    )
    white = whiten(spectra).reshape(day_dev, ch_dev, seg_count, 2 * F)
    own_index = lax.axis_index("chan")
    first_slot = pair_slots[:, 0]
    second_slot = pair_slots[:, 1]
    wanted = lax.dynamic_index_in_dim(block_requests, own_index, axis=1, keepdims=False)
    outgoing = jnp.take(white, wanted.reshape(-1), axis=1)
    received = lax.all_to_all(outgoing, "chan", split_axis=1, concat_axis=1, tiled=True)
    partial_value = cross_parts(
        jnp.take(received, first_slot, axis=1), jnp.take(received, second_slot, axis=1)
    )
    cross_spec = jnp.sum(partial_value, axis=0)
    norm_scale = 1.0 / math.sqrt(2.0 * day_dev * lax.axis_size("day") * seg_count * F)
    table_lags = lag_table()
    stacked = lax.psum_scatter(cross_spec, "day", scatter_dimension=0, tiled=True)
    lagged = jnp.dot(
        stacked, table_lags, precision=lax.Precision.HIGHEST, preferred_element_type=jnp.float32
    )
    return lagged * norm_scale


def solution(mesh):
    return jax.shard_map(
        body,
        mesh=mesh,
        in_specs=(P("day", "chan", None, None), P(), P("chan", None)),
        out_specs=P(("chan", "day"), None),
        check_vma=False,
    )
```

profile of v0, /device:TPU:1, one launch (start us, length us, event | category | flops | bytes accessed | tf_op | source)
XLA Modules:
  0.0 502.5 jit_solution(11217755634380235130)
XLA Ops:
  6.5 0.0 copy-start
  6.5 0.1 multiply_subtract_fusion
  6.6 1.6 dynamic-slice_reduce_fusion
  8.2 0.1 reshape.84
  8.3 0.1 reshape.82
  8.4 34.5 %multiply_convert_fusion.1 = (bf16[2048,1024]{1,0:T(8,128)(2,1)S(1)}, bf16[2048,1024]{1,0:T(8,128)(2,1)S(1)}) fusion(s32[1024]{0:T(1024)S(1)} %iota_add_fusion, f32[2048]{0:T(1024)S(1)} %get-tuple-element.22, f32[2048]{0:T(1024)S(1)} %get-tuple-element.23), kind=kLoop, calls=%fused_computation.19 | loop fusion | flops 37748736 | bytes 8409088 | tf_op jit(solution)/shard_map/convert.4
  43.0 0.0 copy-done
  43.0 6.7 %multiply_reduce_fusion = (f32[768]{0:T(1024)S(1)}, f32[768,2048]{1,0:T(8,128)S(1)}) fusion(bf16[768,2048]{1,0:T(8,128)(2,1)S(1)} %bitcast.21, bf16[2048,1024]{1,0:T(8,128)(2,1)S(1)} %get-tuple-element.17, bf16[2048,1024]{1,0:T(8,128)(2,1)S(1)} %get-tuple-element.16), kind=kOutput, calls=%fused_computation.23 | convolution fusion | flops 6462372864 | bytes 17828864 | tf_op jit(solution)/shard_map/dot_general | solution.py:55
  49.8 2.4 divide_convert_fusion.1
  52.2 0.3 pad_maximum_fusion
  52.5 7.3 %gather_fusion = bf16[64,2,24,2048]{3,2,1,0:T(8,128)(2,1)} fusion(bf16[2,16,24,2048]{3,2,1,0:T(8,128)(2,1)S(1)} %pad_maximum_fusion, s32[1024]{0:T(1024)S(1)} %pad_clamp_fusion.2), kind=kCustom, calls=%fused_computation.2 | custom fusion | bytes 25166080 | tf_op jit(solution)/shard_map/jit(_take)/gather | solution.py:63
  59.8 10.7 %select_bitcast_fusion = bf16[2,64,24,2048]{3,2,0,1:T(8,128)(2,1)} fusion(bf16[64,2,24,2048]{3,2,1,0:T(8,128)(2,1)} %gather_fusion, pred[64]{0:T(512)(128)(4,1)S(1)} %compare_and_fusion.2), kind=kLoop, calls=%fused_computation.5 | loop fusion | flops 6291456 | bytes 25165888 | tf_op jit(solution)/shard_map/jit(_take)/select_n | solution.py:63
  70.6 0.0 copy-start.2
  70.6 12.3 %all-to-all-start = ((bf16[2,64,24,2048]{3,2,0,1:T(8,128)(2,1)}), bf16[2,64,24,2048]{3,2,0,1:T(8,128)(2,1)}, u32[]{:S(2)}, u32[]{:S(2)}) async-start(bf16[2,64,24,2048]{3,2,0,1:T(8,128)(2,1)} %select_bitcast_fusion), calls=%async_computation | async-start | bytes 25165824 | tf_op jit(solution)/shard_map/all_to_all | solution.py:64
  82.9 0.2 reduce-scatter.2.cloned.1.call-start
  83.1 0.0 copy-done.2
  83.1 280.4 %all-to-all-done = bf16[2,64,24,2048]{3,2,0,1:T(8,128)(2,1)} async-done(((bf16[2,64,24,2048]{3,2,0,1:T(8,128)(2,1)}), bf16[2,64,24,2048]{3,2,0,1:T(8,128)(2,1)}, u32[]{:S(2)}, u32[]{:S(2)}) %all-to-all-start) | async-done | bytes 12582944 | tf_op jit(solution)/shard_map/all_to_all | solution.py:64
  363.5 11.8 %gather_fusion.1 = bf16[64,2,24,2048]{3,2,1,0:T(8,128)(2,1)} fusion(bf16[2,64,24,2048]{3,2,0,1:T(8,128)(2,1)} %all-to-all-done, s32[1024]{0:T(1024)S(1)} %get-tuple-element.25), kind=kCustom, calls=%fused_computation.clone | custom fusion | bytes 25166080 | tf_op jit(solution)/shard_map/jit(_take)/gather | solution.py:66
  375.3 14.1 %bitcast_convert_fusion.1 = f32[2,64,24,2048]{3,2,0,1:T(8,128)} fusion(bf16[64,2,24,2048]{3,2,1,0:T(8,128)(2,1)} %gather_fusion.1, pred[64]{0:T(512)(128)(4,1)S(1)} %get-tuple-element.8), kind=kLoop, calls=%fused_computation.4 | loop fusion | flops 12582912 | bytes 37748800 | tf_op jit(solution)/shard_map/convert_element_type | solution.py:44
  389.4 11.8 %gather_fusion.2 = bf16[64,2,24,2048]{3,2,1,0:T(8,128)(2,1)} fusion(bf16[2,64,24,2048]{3,2,0,1:T(8,128)(2,1)} %all-to-all-done, s32[1024]{0:T(1024)S(1)} %get-tuple-element.24), kind=kCustom, calls=%fused_computation.1.clone | custom fusion | bytes 25166080 | tf_op jit(solution)/shard_map/jit(_take)/gather | solution.py:66
  401.2 14.1 %bitcast_convert_fusion = f32[2,64,24,2048]{3,2,0,1:T(8,128)} fusion(bf16[64,2,24,2048]{3,2,1,0:T(8,128)(2,1)} %gather_fusion.2, pred[64]{0:T(512)(128)(4,1)S(1)} %get-tuple-element.18), kind=kLoop, calls=%fused_computation.3 | loop fusion | flops 12582912 | bytes 37748800 | tf_op jit(solution)/shard_map/convert_element_type | solution.py:45
  415.3 0.0 copy-start.1
  415.3 21.0 %add_reduce_fusion = (f32[2,64,1024]{2,0,1:T(2,128)S(1)}, f32[2,64,1024]{2,0,1:T(2,128)S(1)}) fusion(f32[2,64,24,2048]{3,2,0,1:T(8,128)} %bitcast_convert_fusion, f32[2,64,24,2048]{3,2,0,1:T(8,128)} %bitcast_convert_fusion.1), kind=kLoop, calls=%fused_computation.7 | loop fusion | flops 24903680 | bytes 51380224 | tf_op jit(solution)/shard_map/reduce_sum | solution.py:48
  436.4 2.2 maximum_reduce_fusion
  438.6 0.0 reduce-scatter.2.cloned.1.call-update
  438.6 5.8 %fusion.23 = (f32[1024,256]{1,0:T(8,128)}, f32[1024,256]{1,0:T(8,128)}) fusion(s32[256]{0:T(256)S(1)} %iota_add_fusion.1, s32[1024]{0:T(1024)S(1)} %iota_add_fusion), kind=kLoop, calls=%fused_computation.44 | loop fusion | flops 3932160 | bytes 2102272 | tf_op jit(solution)/shard_map/cos | solution.py:30
  444.4 48.1 %reduce-scatter.2.cloned.1.call-done = f32[8,2048]{1,0:T(8,128)} async-done(((f32[64,2048]{1,0:T(8,128)}), f32[8,2048]{1,0:T(8,128)}) %reduce-scatter.2.cloned.1.call-update) | async-done | bytes 65552 | tf_op jit(solution)/shard_map/reduce_scatter | solution.py:71
  492.6 3.1 fusion.17
  495.7 0.0 copy-done.1
  (8 shorter events, 0.0 us)
Async XLA Ops:
  6.5 36.4 %copy-start = (bf16[2,16,24,2048]{3,2,1,0:T(8,128)(2,1)S(1)}, bf16[2,16,24,2048]{3,2,1,0:T(8,128)(2,1)}, u32[]{:S(2)}) copy-start(bf16[2,16,24,2048]{3,2,1,0:T(8,128)(2,1)} %param.5) | copy-start | bytes 9437188
  70.6 12.5 %copy-start.2 = (s32[64,2]{0,1:T(2,128)S(1)}, s32[64,2]{0,1:T(2,128)}, u32[]{:S(2)}) copy-start(s32[64,2]{0,1:T(2,128)} %param.7) | copy-start | bytes 1540
  70.6 293.0 %all-to-all-start = ((bf16[2,64,24,2048]{3,2,0,1:T(8,128)(2,1)}), bf16[2,64,24,2048]{3,2,0,1:T(8,128)(2,1)}, u32[]{:S(2)}, u32[]{:S(2)}) async-start(bf16[2,64,24,2048]{3,2,0,1:T(8,128)(2,1)} %select_bitcast_fusion), calls=%async_computation | async-start | bytes 25165824 | tf_op jit(solution)/shard_map/all_to_all | solution.py:64
  82.9 409.7 %reduce-scatter.2.cloned.1.call-start = ((), (), s32[]{:S(2)}) async-start(), calls=%async_computation.2 | async-start | bytes 589824 | tf_op jit(solution)/shard_map/reduce_scatter | solution.py:71
  415.3 80.3 %copy-start.1 = (bf16[2,16,24,2048]{3,2,1,0:T(8,128)(2,1)S(1)}, bf16[2,16,24,2048]{3,2,1,0:T(8,128)(2,1)}, u32[]{:S(2)}) copy-start(bf16[2,16,24,2048]{3,2,1,0:T(8,128)(2,1)} %param.5) | copy-start | bytes 9437188
Sparse Core Ops, SparseCore 0:
  438.7 53.7 reduce-scatter.1
where the time goes:
time: 504 us; the launch traced here: 503 us
  waiting for transfers between devices  329 us (65%)
  other arithmetic  105 us (21%)
  local copies, waits for them, and re-layouts  32.7 us (6%)
  between operations  13.5 us (3%)
  starting transfers between devices  12.5 us (2%)
  matrix products  9.83 us (2%)
    all_to_all x1, waiting for transfers between devices, body(): lax.all_to_all(outgoing, 'chan', split_axis=1, concat_axis=1, tiled=True)  280 us
    reduce_scatter x1, waiting for transfers between devices, body(): lax.psum_scatter(cross_spec, 'day', scatter_dimension=0, tiled=True)  48.1 us
    another operation x2, other arithmetic  37 us
    reduce_sum x1, other arithmetic, cross_parts(): real_part = jnp.sum(left_real * right_real + left_imag * right_imag, axis=2)  21 us
    convert_element_type x1, other arithmetic, cross_parts(): left_full = left_spec.astype(jnp.float32)  14.1 us
    convert_element_type x1, other arithmetic, cross_parts(): right_full = right_spec.astype(jnp.float32)  14.1 us
    all_to_all x1, starting transfers between devices, body(): lax.all_to_all(outgoing, 'chan', split_axis=1, concat_axis=1, tiled=True)  12.3 us
    gather x1, local copies, waits for them, and re-layouts, body(): jnp.take(received, second_slot, axis=1)  11.8 us
  transfers between devices with their start and end apart: 2, of which 2 were waited for; matrix products, arithmetic and copies ran while one was open for 1% of the time, Pallas kernels for 0%

commit v1 on v0

v1 whole, which is shorter than its diff:
```python
import math

import jax
import jax.numpy as jnp
import numpy as np
from jax import lax
from jax.experimental import pallas as pl
from jax.experimental.pallas import tpu as pltpu
from jax.sharding import PartitionSpec as P

L = 2048
F = 1024
LAGS = 256
MESH = pl.DeviceIdType.MESH
NC = 32
BINS = F // NC
NU = NC // 4
NJ = 3
SEG = 8
CH = 16
ROWS = CH * SEG
ND = 8


def forward_blocks():
    n = np.arange(L, dtype=np.int64)[:, None]
    k = np.arange(1, F + 1, dtype=np.int64)[None, :]
    phase = (n * k % L).astype(np.float32) * np.float32(2.0 * math.pi / L)
    taper = np.float32(0.5) - np.float32(0.5) * np.cos(
        np.arange(L, dtype=np.float32) * np.float32(2.0 * math.pi / L)
    )
    real = (taper[:, None] * np.cos(phase)).reshape(L, NU, 4, BINS)
    imag = (-taper[:, None] * np.sin(phase)).reshape(L, NU, 4, BINS)
    both = np.stack([real, imag], axis=2).reshape(L, NU, 256)
    return np.ascontiguousarray(both.transpose(1, 0, 2)).astype(jnp.bfloat16)


def lag_rows():
    k = np.arange(1, F + 1, dtype=np.int64)[:, None]
    t = np.arange(LAGS, dtype=np.int64)[None, :] - LAGS // 2
    phase = (k * t % L).astype(np.float32) * np.float32(2.0 * math.pi / L)
    both = np.stack([np.cos(phase).reshape(NC, BINS, LAGS), -np.sin(phase).reshape(NC, BINS, LAGS)], axis=1)
    both = both.reshape(2 * F, LAGS).astype(np.float32)
    high = both.astype(jnp.bfloat16)
    return np.stack([high, (both - high.astype(np.float32)).astype(jnp.bfloat16)])


def swap(rows, even):
    return jnp.where(even, pltpu.roll(rows, 96, 1), pltpu.roll(rows, 32, 1))


def kernel(
    req, slots, x_hbm, tab_hbm, lag_hbm, out,
    xv, xs, tab, spec, send, recv, lag, mine_s, mine_v, index_v, index, plain, turned, acc1, acc2,
    day_send, day_recv, own_send, own_recv, lhs,
    x_sem, tab_sem, lag_sem, send_sem, recv_sem, index_send_sem, index_recv_sem, smem_sem,
    day_send_sem, day_recv_sem, own_send_sem, own_recv_sem,
):
    me = lax.axis_index("chan")
    day = lax.axis_index("day")
    my_u = me // 4
    lane = lax.broadcasted_iota(jnp.int32, (ROWS, 128), 1)
    even = lane % 64 < 32
    low = lane < 64

    x_copy = pltpu.make_async_copy(x_hbm, xv, x_sem)
    x_copy.start()

    def tab_copy(step):
        u = lax.rem(my_u + step, NU)
        return pltpu.make_async_copy(tab_hbm.at[u], tab.at[u], tab_sem.at[u])

    @pl.loop(0, NU)
    def _(step):
        tab_copy(step).start()

    lag_copy = pltpu.make_async_copy(lag_hbm, lag, lag_sem)
    lag_copy.start()

    barrier = pltpu.get_barrier_semaphore()

    @pl.loop(1, NC)
    def _(i):
        pl.semaphore_signal(
            barrier, inc=1, device_id=(lax.rem(me + i, NC), day), device_id_type=MESH
        )

    @pl.loop(1, ND)
    def _(i):
        pl.semaphore_signal(
            barrier, inc=1, device_id=(me, lax.rem(day + i, ND)), device_id_type=MESH
        )

    @pl.loop(0, 64)
    def _(i):
        for k in range(2):
            slot = slots[k, i]
            source = slot >> 1
            mine_s[k, i] = source * CH + req[me, slot & 1, source]

    mine_copy = pltpu.make_async_copy(mine_s, mine_v, smem_sem)
    mine_copy.start()

    x_copy.wait()

    @pl.loop(0, 16)
    def _(i):
        rows = xv[pl.ds(pl.multiple_of(i * 48, 16), 48), :].astype(jnp.float32).reshape(2, NJ, SEG, L)
        for j in range(NJ):
            xs[j, pl.ds(pl.multiple_of(i * 16, 16), 16), :] = (
                rows[:, j].reshape(16, L).astype(jnp.bfloat16)
            )

    def block_copy(j, to):
        return pltpu.make_async_remote_copy(
            src_ref=send.at[j, to],
            dst_ref=recv.at[j, me],
            send_sem=send_sem.at[j],
            recv_sem=recv_sem.at[j, me],
            device_id=(to, day),
            device_id_type=MESH,
        )

    def index_copy(to):
        return pltpu.make_async_remote_copy(
            src_ref=mine_v,
            dst_ref=index_v.at[me],
            send_sem=index_send_sem,
            recv_sem=index_recv_sem,
            device_id=(to, day),
            device_id_type=MESH,
        )

    for j in range(NJ):

        def transform(step, total):
            u = lax.rem(my_u + step, NU)
            if j == 0:
                tab_copy(step).wait()
            y = jnp.dot(xs[j], tab[u], preferred_element_type=jnp.float32)
            spec[u] = y
            return total + (y[:, :128] * y[:, :128] + y[:, 128:] * y[:, 128:])

        total = lax.fori_loop(0, NU, transform, jnp.zeros((2 * ROWS, 128), jnp.float32))
        floor = jnp.sum(total, axis=-1, keepdims=True) * (0.02 / (2 * F)) + 1e-06

        if j == 0:
            pl.semaphore_wait(barrier, NC - 1 + ND - 1)

        @pl.loop(0, NU)
        def _(step):
            u = lax.rem(my_u + step, NU)
            parts = []
            for d in range(2):
                real = spec[u, d * ROWS : (d + 1) * ROWS, :128]
                imag = spec[u, d * ROWS : (d + 1) * ROWS, 128:]
                scale = lax.rsqrt(real * real + imag * imag + floor[d * ROWS : (d + 1) * ROWS])
                real, imag = real * scale, swap(imag * scale, even)
                if d == 1:
                    real, imag = pltpu.roll(real, 64, 1), pltpu.roll(imag, 64, 1)
                parts += [jnp.where(even, real, imag), jnp.where(even, imag, real)]
            a, b, c, e = parts
            send[j, 4 * u + 0] = jnp.where(low, a, c).astype(jnp.bfloat16)
            send[j, 4 * u + 1] = jnp.where(low, b, e).astype(jnp.bfloat16)
            send[j, 4 * u + 2] = jnp.where(low, c, a).astype(jnp.bfloat16)
            send[j, 4 * u + 3] = jnp.where(low, e, b).astype(jnp.bfloat16)

            @pl.loop(0, 4)
            def _(q):
                to = 4 * u + q

                @pl.when(to != me)
                def _():
                    block_copy(j, to).start()

        if j == 0:
            mine_copy.wait()
            index_v[me] = mine_v[...]

            @pl.loop(1, NC)
            def _(i):
                index_copy(lax.rem(me + i, NC)).start()

    others = pl.ds(0, NC - 1)
    pltpu.make_async_copy(index_v.at[others], index_v.at[others], index_recv_sem).wait()
    index_to_smem = pltpu.make_async_copy(index_v, index, smem_sem)
    index_to_smem.start()
    index_to_smem.wait()

    def arrive(j, to):
        @pl.loop(0, NC)
        def _(i):
            source = lax.rem(lax.rem(my_u - i // 4 + NU, NU) * 4 + lax.rem(i, 4), NC)
            at = pl.ds(pl.multiple_of(source * CH, CH), CH)

            def store(rows):
                rows = rows.astype(jnp.float32)
                plain[to, at] = rows.reshape(CH, SEG, 128)
                turned[to, at] = swap(rows, even).reshape(CH, SEG, 128)

            @pl.when(source != me)
            def _():
                pltpu.make_async_copy(
                    send.at[j, source], recv.at[j, source], recv_sem.at[j, source]
                ).wait()
                store(recv[j, source])

            @pl.when(source == me)
            def _():
                store(send[j, me])

    sign = jnp.where(even, -1.0, 1.0) * (1 - 2 * lax.rem(me, 2)).astype(jnp.float32)

    def group(dd, chunks):
        @pl.loop(0, NC)
        def _(o):
            for r in range(8):
                first, second = index[o, 0, dd * 8 + r], index[o, 1, dd * 8 + r]
                one = two = None
                for j in range(chunks):
                    a = plain[j, first]
                    b, c = a * plain[j, second], a * turned[j, second]
                    one, two = (b, c) if j == 0 else (one + b, two + c)
                at = pl.ds(pl.multiple_of((o * 8 + r) * 8, 8), 8)
                acc1[at, :] = one
                acc2[at, :] = two

        folded = []
        for half in range(2):
            for k, acc in enumerate((acc1, acc2)):
                total = acc[pl.ds(half * 1024, ROWS, stride=8), :]
                for s in range(1, 8):
                    total = total + acc[pl.ds(half * 1024 + s, ROWS, stride=8), :]
                if k == 1:
                    total = total * sign
                total = total + pltpu.roll(total, 64, 1)
                folded.append(total + pltpu.roll(total, 32, 1))
        re_lo, im_lo, re_hi, im_hi = folded
        return jnp.where(low, jnp.where(even, re_lo, im_lo), jnp.where(even, re_hi, im_hi))

    arrive(0, 0)
    arrive(1, 1)

    @pl.loop(0, ND)
    def _(dd):
        day_send[dd] = group(dd, 2)

    arrive(2, 0)

    def day_copy(to):
        return pltpu.make_async_remote_copy(
            src_ref=day_send.at[to],
            dst_ref=day_recv.at[day],
            send_sem=day_send_sem,
            recv_sem=day_recv_sem.at[day],
            device_id=(me, to),
            device_id_type=MESH,
        )

    @pl.loop(1, ND + 1)
    def _(i):
        dd = lax.rem(day + i, ND)
        day_send[dd] = day_send[dd] + group(dd, 1)

        @pl.when(dd != day)
        def _():
            day_copy(dd).start()

    total = day_send[day]
    own_send[...] = total.reshape(16, 8, 128)

    @pl.loop(1, ND)
    def _(i):
        source = lax.rem(day - i + ND, ND)
        pltpu.make_async_copy(day_send.at[source], day_recv.at[source], day_recv_sem.at[source]).wait()
        own_send[...] = own_send[...] + day_recv[source].reshape(16, 8, 128)

    def own_copy(to):
        return pltpu.make_async_remote_copy(
            src_ref=own_send.at[lax.rem(to, 16)],
            dst_ref=own_recv.at[me],
            send_sem=own_send_sem,
            recv_sem=own_recv_sem,
            device_id=(to, day),
            device_id_type=MESH,
        )

    @pl.loop(1, NC)
    def _(i):
        own_copy(lax.rem(me + i, NC)).start()

    own_recv[me] = own_send[lax.rem(me, 16)]

    pltpu.make_async_copy(own_recv.at[others], own_recv.at[others], own_recv_sem).wait()

    upper = (jnp.zeros((8, 128), jnp.int32) + me) >= 16
    narrow = low[:8]
    for t in range(16):
        pair = []
        for s in (2 * t, 2 * t + 1):
            v = own_recv[s]
            turned_v = pltpu.roll(v, 64, 1)
            pair.append(jnp.where(upper, turned_v, v) if s % 2 == 0 else jnp.where(upper, v, turned_v))
        value = jnp.where(narrow, pair[0], pair[1])
        high = value.astype(jnp.bfloat16).astype(jnp.float32)
        lhs[:, t * 128 : (t + 1) * 128] = jnp.concatenate([high, value - high], axis=0).astype(jnp.bfloat16)

    lag_copy.wait()
    lagged = jnp.dot(lhs[...], lag[0], preferred_element_type=jnp.float32) + jnp.dot(
        lhs[...], lag[1], preferred_element_type=jnp.float32
    )
    out[...] = (lagged[:8] + lagged[8:]) * (1.0 / math.sqrt(2.0 * 16 * 24 * F))

    for j in range(NJ):
        pltpu.make_async_copy(send.at[j, others], recv.at[j, others], send_sem.at[j]).wait()
    pltpu.make_async_copy(index_v.at[others], index_v.at[others], index_send_sem).wait()
    pltpu.make_async_copy(own_recv.at[others], own_recv.at[others], own_send_sem).wait()
    days = pl.ds(0, ND - 1)
    pltpu.make_async_copy(day_send.at[days], day_recv.at[days], day_send_sem).wait()


def body(segment_records, block_requests, pair_slots):
    bf16, f32, i32 = jnp.bfloat16, jnp.float32, jnp.int32
    dma = pltpu.SemaphoreType.DMA
    return pl.pallas_call(
        kernel,
        out_shape=jax.ShapeDtypeStruct((8, LAGS), f32),
        in_specs=[
            pl.BlockSpec(memory_space=pltpu.SMEM),
            pl.BlockSpec(memory_space=pltpu.SMEM),
            pl.BlockSpec(memory_space=pl.ANY),
            pl.BlockSpec(memory_space=pl.ANY),
            pl.BlockSpec(memory_space=pl.ANY),
        ],
        out_specs=pl.BlockSpec(memory_space=pltpu.VMEM),
        scratch_shapes=[
            pltpu.VMEM((768, L), bf16),
            pltpu.VMEM((NJ, 256, L), bf16),
            pltpu.VMEM((NU, L, 256), bf16),
            pltpu.VMEM((NU, 256, 256), f32),
            pltpu.VMEM((NJ, NC, ROWS, 128), bf16),
            pltpu.VMEM((NJ, NC, ROWS, 128), bf16),
            pltpu.VMEM((2, 2 * F, LAGS), bf16),
            pltpu.SMEM((2, 64), i32),
            pltpu.VMEM((2, 64), i32),
            pltpu.VMEM((NC, 2, 64), i32),
            pltpu.SMEM((NC, 2, 64), i32),
            pltpu.VMEM((2, NC * CH, SEG, 128), f32),
            pltpu.VMEM((2, NC * CH, SEG, 128), f32),
            pltpu.VMEM((2048, 128), f32),
            pltpu.VMEM((2048, 128), f32),
            pltpu.VMEM((ND, ROWS, 128), f32),
            pltpu.VMEM((ND, ROWS, 128), f32),
            pltpu.VMEM((16, 8, 128), f32),
            pltpu.VMEM((NC, 8, 128), f32),
            pltpu.VMEM((16, 2 * F), bf16),
            dma, dma((NU,)), dma, dma((NJ,)), dma((NJ, NC)), dma, dma, dma,
            dma, dma((ND,)), dma, dma,
        ],
        compiler_params=pltpu.CompilerParams(
            collective_id=0, has_side_effects=True, vmem_limit_bytes=60 * 2**20
        ),
        name="correlate",
    )(
        block_requests.transpose(0, 2, 1),
        pair_slots.T,
        segment_records.reshape(768, L),
        jnp.asarray(forward_blocks()),
        jnp.asarray(lag_rows()),
    )


def solution(mesh):
    return jax.shard_map(
        body,
        mesh=mesh,
        in_specs=(P("day", "chan", None, None), P(), P("chan", None)),
        out_specs=P(("chan", "day"), None),
        check_vma=False,
    )
```

time: 504 us -> 110 us (0.22)
  waiting for transfers between devices: 329 us -> 0 us
  Pallas kernels: 0 us -> 108 us
  other arithmetic: 105 us -> 0 us
  local copies, waits for them, and re-layouts: 32.7 us -> 1.3 us
  between operations: 13.5 us -> 0.01 us
  starting transfers between devices: 12.5 us -> 0 us
  matrix products: 9.83 us -> 0 us
    all_to_all x1 -> x0, waiting for transfers between devices: 280 us -> none  [body(): lax.all_to_all(outgoing, 'chan', split_axis=1, concat_axis=1, tiled=True)]
    pallas_call x0 -> x1, Pallas kernels: none -> 108 us  [body(): pl.pallas_call(kernel, out_shape=jax.ShapeDtypeStruct((8, LAGS), f32), in...]
    reduce_scatter x1 -> x0, waiting for transfers between devices: 48.1 us -> none  [body(): lax.psum_scatter(cross_spec, 'day', scatter_dimension=0, tiled=True)]
    another operation x2 -> x0, other arithmetic: 37 us -> none
    gather x3 -> x0, local copies, waits for them, and re-layouts: 30.9 us -> none  [the longest x1 11.8 us: body(): jnp.take(received, second_slot, axis=1)]
    convert_element_type x2 -> x0, other arithmetic: 28.2 us -> none  [the longest x1 14.1 us: cross_parts(): left_full = left_spec.astype(jnp.float32)]
    reduce_sum x2 -> x0, other arithmetic: 23.2 us -> none  [the longest x1 21 us: cross_parts(): real_part = jnp.sum(left_real * right_real + left_imag * right_imag, axis=2)]
    all_to_all x1 -> x0, starting transfers between devices: 12.3 us -> none  [body(): lax.all_to_all(outgoing, 'chan', split_axis=1, concat_axis=1, tiled=True)]
  transfers between devices with their start and end apart: 2 -> 0, of which waited for: 2 -> 0; matrix products, arithmetic and copies ran while one was open for 1% -> 0% of each run, Pallas kernels for 0% -> 0%
where the time goes in v1:
time: 110 us
  Pallas kernels  108 us (98%)
  local copies, waits for them, and re-layouts  1.3 us (1%)
    pallas_call x1, Pallas kernels, body(): pl.pallas_call(kernel, out_shape=jax.ShapeDtypeStruct((8, LAGS), f32), in...  108 us

profile of v1, /device:TPU:1, one launch (start us, length us, event | category | flops | bytes accessed | tf_op | source)
XLA Modules:
  0.0 109.7 jit_solution(6034412559759464853)
XLA Ops:
  0.0 108.4 %correlate.1 = f32[8,256]{1,0:T(8,128)} custom-call(s32[32,2,32]{2,1,0:T(2,128)} %bitcast.4, s32[2,64]{1,0:T(2,128)} %bitcast.5, bf16[768,2048]{1,0:T(8,128)(2,1)} %bitcast.3, bf16[8,2048,256]{2,1,0:T(8,128)(2,1)} %constant.4.clone.tab_hbm, bf16[2,2048,256]{2,1,0:T(8,128)(2,1)} %constant.5.clone.lag_hbm), custom_call_target="tpu_custom_call" | custom-call | tf_op jit(solution)/shard_map/correlate/pallas_call | solution.py:325
  108.4 1.3 %copy.7 = f32[8,256]{1,0:T(8,128)} copy(f32[8,256]{1,0:T(8,128)} %correlate.1) | data formatting | bytes 16384

commit v2 on v1

v2 whole, which is shorter than its diff:
```python
import math

import jax
import jax.numpy as jnp
import numpy as np
from jax import lax
from jax.experimental import pallas as pl
from jax.experimental.pallas import tpu as pltpu
from jax.sharding import PartitionSpec as P

L = 2048
F = 1024
LAGS = 256
MESH = pl.DeviceIdType.MESH
NC = 32
BINS = F // NC
NU = NC // 4
NJ = 3
SEG = 8
CH = 16
ROWS = CH * SEG
ND = 8


def forward_blocks():
    n = np.arange(L, dtype=np.int64)[:, None]
    k = np.arange(1, F + 1, dtype=np.int64)[None, :]
    phase = (n * k % L).astype(np.float32) * np.float32(2.0 * math.pi / L)
    taper = np.float32(0.5) - np.float32(0.5) * np.cos(
        np.arange(L, dtype=np.float32) * np.float32(2.0 * math.pi / L)
    )
    real = (taper[:, None] * np.cos(phase)).reshape(L, NU, 4, BINS)
    imag = (-taper[:, None] * np.sin(phase)).reshape(L, NU, 4, BINS)
    both = np.stack([real, imag], axis=2).reshape(L, NU, 256)
    return np.ascontiguousarray(both.transpose(1, 0, 2)).astype(jnp.bfloat16)


def taper_rows():
    n = np.arange(L, dtype=np.float32)
    taper = np.float32(0.5) - np.float32(0.5) * np.cos(n * np.float32(2.0 * math.pi / L))
    return np.broadcast_to(taper, (8, L)).copy()


def lag_rows():
    k = np.arange(1, F + 1, dtype=np.int64)[:, None]
    t = np.arange(LAGS, dtype=np.int64)[None, :] - LAGS // 2
    phase = (k * t % L).astype(np.float32) * np.float32(2.0 * math.pi / L)
    shape = (NC // 2, 2, BINS, LAGS)
    both = np.stack([np.cos(phase).reshape(shape), -np.sin(phase).reshape(shape)], axis=1)
    both = both.reshape(2 * F, LAGS).astype(np.float32)
    high = both.astype(jnp.bfloat16)
    return np.stack([high, (both - high.astype(np.float32)).astype(jnp.bfloat16)])


def alternate(count, step):
    return count // 2 + (1 - 2 * lax.rem(step, 2)) * ((step + 1) // 2)


def kernel(
    req_hbm, slots_hbm, x_hbm, taper_hbm, tab_hbm, lag_hbm, out,
    req, slots, xv, xs, taper, squares, sums, tab, spec, send, recv, lag, mine_s, mine_v, index_v, index_s, index, forms, acc,
    day_send, day_recv, last_send, last_recv, own_send, own_recv, lhs,
    in_sem, x_sem, taper_sem, tab_sem, lag_sem, send_sem, recv_sem, index_send_sem, index_recv_sem, smem_sem,
    day_send_sem, day_recv_sem, last_send_sem, last_recv_sem, own_send_sem, own_recv_sem,
):
    me = lax.axis_index("chan")
    day = lax.axis_index("day")
    my_u = me // 4
    lane = lax.broadcasted_iota(jnp.int32, (ROWS, 128), 1)
    even = lane % 64 < 32
    low = lane < 64

    def peer(step):
        y = lax.rem(me // 8 + alternate(4, lax.rem(step, 4)), 4)
        z = lax.rem(lax.rem(me, 8) + alternate(8, step // 4), 8)
        return y * 8 + z

    x_copy = pltpu.make_async_copy(x_hbm, xv, x_sem)
    x_copy.start()
    taper_copy = pltpu.make_async_copy(taper_hbm, taper, taper_sem)
    taper_copy.start()
    slots_copy = pltpu.make_async_copy(slots_hbm, slots, in_sem.at[0])
    slots_copy.start()
    req_copy = pltpu.make_async_copy(req_hbm, req, in_sem.at[1])
    req_copy.start()

    barrier = pltpu.get_barrier_semaphore()

    @pl.loop(0, NC - 1)
    def _(i):
        pl.semaphore_signal(barrier, inc=1, device_id=(peer(i), day), device_id_type=MESH)

    @pl.loop(1, ND)
    def _(i):
        pl.semaphore_signal(
            barrier, inc=1, device_id=(me, lax.rem(day + i, ND)), device_id_type=MESH
        )

    def tab_copy(step):
        u = lax.rem(my_u + step, NU)
        return pltpu.make_async_copy(tab_hbm.at[u], tab.at[u], tab_sem.at[u])

    @pl.loop(0, NU)
    def _(step):
        tab_copy(step).start()

    lag_copy = pltpu.make_async_copy(lag_hbm, lag, lag_sem)
    lag_copy.start()

    slots_copy.wait()
    req_copy.wait()

    @pl.loop(0, 64)
    def _(i):
        for k in range(2):
            slot = slots[k, i]
            source = slot >> 1
            mine_s[k, i] = (source * CH + req[me, slot & 1, source]) * 4

    mine_copy = pltpu.make_async_copy(mine_s, mine_v, smem_sem)
    mine_copy.start()

    taper_copy.wait()
    x_copy.wait()

    def gather_rows(chunks):
        @pl.loop(0, 16)
        def _(i):
            rows = xv[pl.ds(pl.multiple_of(i * 48, 16), 48), :].astype(jnp.float32)
            rows = rows.reshape(2, NJ, SEG, L)
            at = pl.ds(pl.multiple_of(i * 16, 16), 16)
            for j in chunks:
                xs[j, at, :] = rows[:, j].reshape(16, L).astype(jnp.bfloat16)
                for half in range(2):
                    tapered = rows[half, j] * taper[...]
                    square = plain = None
                    for t in range(L // 128):
                        part = tapered[:, t * 128 : (t + 1) * 128]
                        square = part * part if t == 0 else square + part * part
                        plain = part if t == 0 else plain + part
                    low_at = pl.ds(pl.multiple_of(i * 16 + half * 8, 8), 8)
                    squares[j, low_at, :] = square
                    sums[j, low_at, :] = plain

    gather_rows((0,))

    def block_copy(j, to):
        return pltpu.make_async_remote_copy(
            src_ref=send.at[j, to],
            dst_ref=recv.at[j, me],
            send_sem=send_sem.at[j],
            recv_sem=recv_sem.at[j, me],
            device_id=(to, day),
            device_id_type=MESH,
        )

    def index_copy(to):
        return pltpu.make_async_remote_copy(
            src_ref=mine_v,
            dst_ref=index_v.at[me],
            send_sem=index_send_sem,
            recv_sem=index_recv_sem,
            device_id=(to, day),
            device_id_type=MESH,
        )

    def floor_of(j):
        odd_lane = lax.broadcasted_iota(jnp.int32, (2 * ROWS, 128), 1) % 2 == 1
        total = jnp.sum(squares[j], axis=-1, keepdims=True)
        odd = jnp.sum(jnp.where(odd_lane, sums[j], 0.0), axis=-1, keepdims=True)
        plain = jnp.sum(jnp.where(odd_lane, 0.0, sums[j]), axis=-1, keepdims=True)
        power = jnp.maximum(1024.0 * total - 2.0 * odd * plain, 0.0)
        return power * (0.02 / (2 * F)) + 1e-06

    for j in range(NJ):
        floor = floor_of(j)

        def whiten(step):
            u = lax.rem(my_u + step, NU)
            if j == 0:
                tab_copy(step).wait()
            spec[...] = jnp.dot(xs[j], tab[u], preferred_element_type=jnp.float32)
            parts = []
            for d in range(2):
                real = spec[d * ROWS : (d + 1) * ROWS, :128]
                imag = spec[d * ROWS : (d + 1) * ROWS, 128:]
                scale = lax.rsqrt(real * real + imag * imag + floor[d * ROWS : (d + 1) * ROWS])
                parts.append((real * scale, imag * scale))
            (re0, im0), (re1, im1) = parts
            re1 = jnp.where(even, pltpu.roll(re1, 96, 1), pltpu.roll(re1, 32, 1))
            im0 = pltpu.roll(im0, 64, 1)
            im1 = jnp.where(even, pltpu.roll(im1, 32, 1), pltpu.roll(im1, 96, 1))
            a, b = jnp.where(even, re0, re1), jnp.where(even, re1, re0)
            c, e = jnp.where(even, im0, im1), jnp.where(even, im1, im0)
            send[j, 4 * u + 0] = jnp.where(low, a, c).astype(jnp.bfloat16)
            send[j, 4 * u + 1] = jnp.where(low, b, e).astype(jnp.bfloat16)
            send[j, 4 * u + 2] = jnp.where(low, c, a).astype(jnp.bfloat16)
            send[j, 4 * u + 3] = jnp.where(low, e, b).astype(jnp.bfloat16)

        def send_four(step):
            u = lax.rem(my_u + step, NU)

            @pl.loop(0, 4)
            def _(q):
                to = 4 * u + q

                @pl.when(to != me)
                def _():
                    block_copy(j, to).start()

        whiten(0)
        if j == 0:
            pl.semaphore_wait(barrier, NC - 1 + ND - 1)
        send_four(0)

        @pl.loop(1, NU)
        def _(step):
            whiten(step)
            send_four(step)

        if j == 0:
            mine_copy.wait()
            index_v[me] = mine_v[...]

            @pl.loop(0, NC - 1)
            def _(i):
                index_copy(peer(i)).start()

            gather_rows((1, 2))

    others = pl.ds(0, NC - 1)
    pltpu.make_async_copy(index_v.at[others], index_v.at[others], index_recv_sem).wait()
    index_to_smem = pltpu.make_async_copy(index_v, index_s, smem_sem)
    index_to_smem.start()
    index_to_smem.wait()

    @pl.loop(0, ND)
    def _(dd):
        @pl.loop(0, NC)
        def _(o):
            for r in range(8):
                for k in range(2):
                    index[dd * 512 + o * 16 + 2 * r + k] = index_s[o, k, dd * 8 + r]

    flip = jnp.where(low, 1.0, -1.0)

    def arrive(j, to):
        @pl.loop(0, NC)
        def _(i):
            source = lax.rem(my_u - i // 4 + NU, NU) * 4 + lax.rem(i, 4)

            def store(rows):
                rows = rows.astype(jnp.float32)
                turned = pltpu.roll(rows, 64, 1)
                four = (jnp.where(low, rows, turned), jnp.where(low, turned, rows), rows * flip, turned)
                for c in range(CH):
                    for k, form in enumerate(four):
                        forms[to, (source * CH + c) * 4 + k] = form[c * SEG : (c + 1) * SEG]

            @pl.when(source != me)
            def _():
                pltpu.make_async_copy(
                    send.at[j, source], recv.at[j, source], recv_sem.at[j, source]
                ).wait()
                store(recv[j, source])

            @pl.when(source == me)
            def _():
                store(send[j, me])

    sign = jnp.where(low, 1.0, 1.0 - 2.0 * (lax.rem(me, 4) // 2).astype(jnp.float32))
    unroll = 32

    def group(dd, chunks):
        @pl.loop(0, 256 // unroll)
        def _(i):
            for r in range(unroll):
                at = dd * 512 + i * (2 * unroll) + 2 * r
                first, second = index[at], index[at + 1]
                total = None
                for j in range(chunks):
                    value = forms[j, first] * forms[j, second + 2]
                    value += forms[j, first + 1] * forms[j, second + 3]
                    total = value if total is None else total + value
                acc[pl.ds(pl.multiple_of((i * unroll + r) * 8, 8), 8), :] = total

        halves = []
        for half in range(2):
            total = acc[pl.ds(half * 1024, ROWS, stride=8), :]
            for s in range(1, 8):
                total = total + acc[pl.ds(half * 1024 + s, ROWS, stride=8), :]
            total = total * sign
            halves.append(total + pltpu.roll(total, 32 if half else 96, 1))
        return jnp.where(even, halves[0], halves[1])

    arrive(0, 0)
    arrive(1, 1)

    def day_copy(to, source, target, send_sem, recv_sem):
        return pltpu.make_async_remote_copy(
            src_ref=source.at[to],
            dst_ref=target.at[day],
            send_sem=send_sem,
            recv_sem=recv_sem.at[day],
            device_id=(me, to),
            device_id_type=MESH,
        )

    def day_at(i):
        x = lax.rem(day // 2 + alternate(4, i // 2), 4)
        return x * 2 + lax.rem(day + 1 + i, 2)

    @pl.loop(0, ND)
    def _(i):
        dd = day_at(i)
        day_send[dd] = group(dd, 2)

        @pl.when(dd != day)
        def _():
            day_copy(dd, day_send, day_recv, day_send_sem, day_recv_sem).start()

    arrive(2, 0)

    @pl.loop(0, ND)
    def _(i):
        dd = day_at(i)
        last = group(dd, 1)

        @pl.when(dd != day)
        def _():
            last_send[dd] = last.astype(jnp.bfloat16)
            day_copy(dd, last_send, last_recv, last_send_sem, last_recv_sem).start()

        @pl.when(dd == day)
        def _():
            own_send[...] = (day_send[day] + last).reshape(16, 8, 128)

    @pl.loop(0, ND - 1)
    def _(i):
        source = day_at(i)
        pltpu.make_async_copy(day_send.at[source], day_recv.at[source], day_recv_sem.at[source]).wait()
        pltpu.make_async_copy(last_send.at[source], last_recv.at[source], last_recv_sem.at[source]).wait()
        value = day_recv[source] + last_recv[source].astype(jnp.float32)
        own_send[...] = own_send[...] + value.reshape(16, 8, 128)

    def own_copy(to):
        return pltpu.make_async_remote_copy(
            src_ref=own_send.at[lax.rem(to, 16)],
            dst_ref=own_recv.at[me],
            send_sem=own_send_sem,
            recv_sem=own_recv_sem,
            device_id=(to, day),
            device_id_type=MESH,
        )

    @pl.loop(0, NC - 1)
    def _(i):
        own_copy(peer(i)).start()

    own_recv[me] = own_send[lax.rem(me, 16)]

    pltpu.make_async_copy(own_recv.at[others], own_recv.at[others], own_recv_sem).wait()

    upper = (jnp.zeros((8, 128), jnp.int32) + me) >= 16
    for t in range(16):
        one, two = own_recv[2 * t], own_recv[2 * t + 1]
        one = jnp.where(upper, pltpu.roll(one, 96, 1), one)
        two = jnp.where(upper, two, pltpu.roll(two, 32, 1))
        value = jnp.where(even[:8], one, two)
        high = value.astype(jnp.bfloat16).astype(jnp.float32)
        lhs[:, t * 128 : (t + 1) * 128] = jnp.concatenate([high, value - high], axis=0).astype(jnp.bfloat16)

    lag_copy.wait()
    lagged = jnp.dot(lhs[...], lag[0], preferred_element_type=jnp.float32) + jnp.dot(
        lhs[...], lag[1], preferred_element_type=jnp.float32
    )
    out[...] = (lagged[:8] + lagged[8:]) * (1.0 / math.sqrt(2.0 * 16 * 24 * F))

    for j in range(NJ):
        pltpu.make_async_copy(send.at[j, others], recv.at[j, others], send_sem.at[j]).wait()
    pltpu.make_async_copy(index_v.at[others], index_v.at[others], index_send_sem).wait()
    pltpu.make_async_copy(own_recv.at[others], own_recv.at[others], own_send_sem).wait()
    days = pl.ds(0, ND - 1)
    pltpu.make_async_copy(day_send.at[days], day_recv.at[days], day_send_sem).wait()
    pltpu.make_async_copy(last_send.at[days], last_recv.at[days], last_send_sem).wait()


def body(segment_records, block_requests, pair_slots):
    bf16, f32, i32 = jnp.bfloat16, jnp.float32, jnp.int32
    dma = pltpu.SemaphoreType.DMA
    return pl.pallas_call(
        kernel,
        out_shape=jax.ShapeDtypeStruct((8, LAGS), f32),
        in_specs=[
            pl.BlockSpec(memory_space=pl.ANY),
            pl.BlockSpec(memory_space=pl.ANY),
            pl.BlockSpec(memory_space=pl.ANY),
            pl.BlockSpec(memory_space=pl.ANY),
            pl.BlockSpec(memory_space=pl.ANY),
            pl.BlockSpec(memory_space=pl.ANY),
        ],
        out_specs=pl.BlockSpec(memory_space=pltpu.VMEM),
        scratch_shapes=[
            pltpu.SMEM((NC, 2, NC), i32),
            pltpu.SMEM((2, 64), i32),
            pltpu.VMEM((768, L), bf16),
            pltpu.VMEM((NJ, 256, L), bf16),
            pltpu.VMEM((8, L), f32),
            pltpu.VMEM((NJ, 256, 128), f32),
            pltpu.VMEM((NJ, 256, 128), f32),
            pltpu.VMEM((NU, L, 256), bf16),
            pltpu.VMEM((256, 256), f32),
            pltpu.VMEM((NJ, NC, ROWS, 128), bf16),
            pltpu.VMEM((NJ, NC, ROWS, 128), bf16),
            pltpu.VMEM((2, 2 * F, LAGS), bf16),
            pltpu.SMEM((2, 64), i32),
            pltpu.VMEM((2, 64), i32),
            pltpu.VMEM((NC, 2, 64), i32),
            pltpu.SMEM((NC, 2, 64), i32),
            pltpu.SMEM((4096,), i32),
            pltpu.VMEM((2, NC * CH * 4, SEG, 128), f32),
            pltpu.VMEM((2048, 128), f32),
            pltpu.VMEM((ND, ROWS, 128), f32),
            pltpu.VMEM((ND, ROWS, 128), f32),
            pltpu.VMEM((ND, ROWS, 128), bf16),
            pltpu.VMEM((ND, ROWS, 128), bf16),
            pltpu.VMEM((16, 8, 128), f32),
            pltpu.VMEM((NC, 8, 128), f32),
            pltpu.VMEM((16, 2 * F), bf16),
            dma((2,)), dma, dma, dma((NU,)), dma, dma((NJ,)), dma((NJ, NC)), dma, dma, dma,
            dma, dma((ND,)), dma, dma((ND,)), dma, dma,
        ],
        compiler_params=pltpu.CompilerParams(
            collective_id=0, has_side_effects=True, vmem_limit_bytes=60 * 2**20
        ),
        name="correlate",
    )(
        block_requests.transpose(0, 2, 1),
        pair_slots.T,
        segment_records.reshape(768, L),
        jnp.asarray(taper_rows()),
        jnp.asarray(forward_blocks()),
        jnp.asarray(lag_rows()),
    )


def solution(mesh):
    return jax.shard_map(
        body,
        mesh=mesh,
        in_specs=(P("day", "chan", None, None), P(), P("chan", None)),
        out_specs=P(("chan", "day"), None),
        check_vma=False,
    )
```

time: 110 us -> 100 us (0.909)
  Pallas kernels: 108 us -> 98.7 us
    pallas_call x1, Pallas kernels: 108 us -> 98.7 us  [body(): pl.pallas_call(kernel, out_shape=jax.ShapeDtypeStruct((8, LAGS), f32), in...]
where the time goes in v2:
time: 100 us
  Pallas kernels  98.7 us (99%)
  local copies, waits for them, and re-layouts  1.3 us (1%)
    pallas_call x1, Pallas kernels, body(): pl.pallas_call(kernel, out_shape=jax.ShapeDtypeStruct((8, LAGS), f32), in...  98.7 us

profile of v2, /device:TPU:1, one launch (start us, length us, event | category | flops | bytes accessed | tf_op | source)
XLA Modules:
  0.0 100.0 jit_solution(2605614398280881933)
XLA Ops:
  0.0 98.7 %correlate.1 = f32[8,256]{1,0:T(8,128)} custom-call(s32[32,2,32]{2,1,0:T(2,128)} %bitcast.4, s32[2,64]{1,0:T(2,128)} %bitcast.5, bf16[768,2048]{1,0:T(8,128)(2,1)} %bitcast.3, f32[8,2048]{1,0:T(8,128)} %constant.6.clone.taper_hbm, bf16[8,2048,256]{2,1,0:T(8,128)(2,1)} %constant.7.clone.tab_hbm, bf16[2,2048,256]{2,1,0:T(8,128)(2,1)} %constant.8.clone.lag_hbm), custom_call_target="tpu_custom_call" | custom-call | tf_op jit(solution)/shard_map/correlate/pallas_call | solution.py:391
  98.7 1.3 %copy.8 = f32[8,256]{1,0:T(8,128)} copy(f32[8,256]{1,0:T(8,128)} %correlate.1) | data formatting | bytes 16384

commit v3 on v2

--- a/solution.py
+++ b/solution.py
@@ -169,8 +169,8 @@
         total = jnp.sum(squares[j], axis=-1, keepdims=True)
         odd = jnp.sum(jnp.where(odd_lane, sums[j], 0.0), axis=-1, keepdims=True)
         plain = jnp.sum(jnp.where(odd_lane, 0.0, sums[j]), axis=-1, keepdims=True)
-        power = jnp.maximum(1024.0 * total - 2.0 * odd * plain, 0.0)
-        return power * (0.02 / (2 * F)) + 1e-06
+        mean = jnp.maximum(0.5 * total - odd * (plain * (1.0 / F)), 0.0)
+        return 0.02 * mean + 1e-06
 
     for j in range(NJ):
         floor = floor_of(j)
@@ -209,11 +209,13 @@
                     block_copy(j, to).start()
 
         whiten(0)
+        whiten(1)
         if j == 0:
             pl.semaphore_wait(barrier, NC - 1 + ND - 1)
         send_four(0)
-
-        @pl.loop(1, NU)
+        send_four(1)
+
+        @pl.loop(2, NU)
         def _(step):
             whiten(step)
             send_four(step)

time: 100 us -> 100 us (level)
  no operation moved by 1% of the time
where the time goes in v3:
time: 100 us; the launch traced here: 99.7 us
  Pallas kernels  98.4 us (98%)
  local copies, waits for them, and re-layouts  1.3 us (1%)
    pallas_call x1, Pallas kernels, body(): pl.pallas_call(kernel, out_shape=jax.ShapeDtypeStruct((8, LAGS), f32), in...  98.4 us

profile of v3, /device:TPU:1, one launch (start us, length us, event | category | flops | bytes accessed | tf_op | source)
XLA Modules:
  0.0 99.7 jit_solution(3479157905327864475)
XLA Ops:
  0.0 98.4 %correlate.1 = f32[8,256]{1,0:T(8,128)} custom-call(s32[32,2,32]{2,1,0:T(2,128)} %bitcast.4, s32[2,64]{1,0:T(2,128)} %bitcast.5, bf16[768,2048]{1,0:T(8,128)(2,1)} %bitcast.3, f32[8,2048]{1,0:T(8,128)} %constant.6.clone.taper_hbm, bf16[8,2048,256]{2,1,0:T(8,128)(2,1)} %constant.7.clone.tab_hbm, bf16[2,2048,256]{2,1,0:T(8,128)(2,1)} %constant.8.clone.lag_hbm), custom_call_target="tpu_custom_call" | custom-call | tf_op jit(solution)/shard_map/correlate/pallas_call | solution.py:393
  98.4 1.3 %copy.8 = f32[8,256]{1,0:T(8,128)} copy(f32[8,256]{1,0:T(8,128)} %correlate.1) | data formatting | bytes 16384

commit v4 on v3

--- a/solution.py
+++ b/solution.py
@@ -376,7 +376,7 @@
     lagged = jnp.dot(lhs[...], lag[0], preferred_element_type=jnp.float32) + jnp.dot(
         lhs[...], lag[1], preferred_element_type=jnp.float32
     )
-    out[...] = (lagged[:8] + lagged[8:]) * (1.0 / math.sqrt(2.0 * 16 * 24 * F))
+    out[...] = lagged[:8] + lagged[8:]
 
     for j in range(NJ):
         pltpu.make_async_copy(send.at[j, others], recv.at[j, others], send_sem.at[j]).wait()
@@ -390,7 +390,7 @@
 def body(segment_records, block_requests, pair_slots):
     bf16, f32, i32 = jnp.bfloat16, jnp.float32, jnp.int32
     dma = pltpu.SemaphoreType.DMA
-    return pl.pallas_call(
+    lagged = pl.pallas_call(
         kernel,
         out_shape=jax.ShapeDtypeStruct((8, LAGS), f32),
         in_specs=[
@@ -444,6 +444,7 @@
         jnp.asarray(forward_blocks()),
         jnp.asarray(lag_rows()),
     )
+    return lagged * (1.0 / math.sqrt(2.0 * 16 * 24 * F))
 
 
 def solution(mesh):

time: 100 us -> 100 us (level)
  other arithmetic: 0 us -> 1.3 us
  local copies, waits for them, and re-layouts: 1.3 us -> 0 us
    mul x0 -> x1, other arithmetic: none -> 1.3 us  [body(): return lagged * (1.0 / math.sqrt(2.0 * 16 * 24 * F))]
    unnamed x1 -> x0, local copies, waits for them, and re-layouts: 1.3 us -> none
where the time goes in v4:
time: 100 us; the launch traced here: 99.7 us
  Pallas kernels  98.4 us (98%)
  other arithmetic  1.3 us (1%)
    pallas_call x1, Pallas kernels, body(): pl.pallas_call(kernel, out_shape=jax.ShapeDtypeStruct((8, LAGS), f32), in...  98.4 us

profile of v4, /device:TPU:1, one launch (start us, length us, event | category | flops | bytes accessed | tf_op | source)
XLA Modules:
  0.0 99.7 jit_solution(1084650135299370339)
XLA Ops:
  0.0 98.4 %correlate.1 = f32[8,256]{1,0:T(8,128)} custom-call(s32[32,2,32]{2,1,0:T(2,128)} %bitcast.4, s32[2,64]{1,0:T(2,128)} %bitcast.5, bf16[768,2048]{1,0:T(8,128)(2,1)} %bitcast.3, f32[8,2048]{1,0:T(8,128)} %constant.8.clone.taper_hbm, bf16[8,2048,256]{2,1,0:T(8,128)(2,1)} %constant.9.clone.tab_hbm, bf16[2,2048,256]{2,1,0:T(8,128)(2,1)} %constant.10.clone.lag_hbm), custom_call_target="tpu_custom_call" | custom-call | tf_op jit(solution)/shard_map/correlate/pallas_call | solution.py:393
  98.4 1.3 %broadcast_multiply_fusion = f32[8,256]{1,0:T(8,128)} fusion(f32[8,256]{1,0:T(8,128)} %correlate.1), kind=kLoop, calls=%fused_computation | loop fusion | flops 2048 | bytes 16384 | tf_op jit(solution)/shard_map/mul | solution.py:447
